TPU v7x, 32 devices: a whole 2x2x4 slice. The times are simulated.
32 devices in a mesh: bl: 8 (over y, x, core), dir: 4 (over z).
Axes of the slice: x: 2, y: 2, z: 4, core: 2. Of those that a mesh axis runs over, the one named last changes fastest.
Arguments:
- visibilities: float32 [8, 16, 2048], P(None, 'dir', 'bl'), may hold values from -24 to 24
- coherencies: bfloat16 [32, 8, 16, 2048], P('dir', None, None, 'bl'), may hold values from -6 to 6
- gain_offsets: float32 [32, 8, 512], P(None, None, 'bl'), may hold values from -1.5 to 1.5
- stations: int32 [2, 2048], P(None, 'bl'), may hold values from 0 to 511, as said below
- solve_order: int32 [32], replicated, may hold values from 0 to 31, each once
- counts: int32 [32], replicated, may hold values from 1 to 2
- damping: int32 [32], replicated, may hold values from 1 to 8
Outputs:
- gains: float32 [32, 8, 512], P(None, None, 'bl')
- residual: float32 [8, 16, 2048], P(None, 'dir', 'bl')
Inputs may be any that keep to these rules, and one draw needn't show every extreme that they name: Each baseline names two different stations. `solve_order`: each direction appears once.
All inputs are finite; a program needn't handle non-finite values.
Results may differ from a plain program's by a relative error of at most 0.0003.
Values may be sent and summed in bfloat16 or wider, within the bound.
No kernel may reach another device: no remote copies, remote signals or barrier semaphores. Data moves between devices by JAX's collectives and lax.ppermute only.
A program may use at most 64 MiB of HBM per device.

v0:
```python
import jax
import jax.numpy as jnp
from jax import lax
from jax.sharding import PartitionSpec as P

LM_ITERS = 2
SOLVED = 4


def from_root(shard, axis, root):
    mine = lax.axis_index(axis) == root
    return lax.psum(jnp.where(mine, shard, jnp.zeros_like(shard)), axis)


def matrix_entry(mat, i, j):
    return (mat[4 * i + 2 * j], mat[4 * i + 2 * j + 1])


def matmul_two(left, right):
    pieces = []
    for i in (0, 1):
        for j in (0, 1):
            left_r0, left_i0 = matrix_entry(left, i, 0)
            left_r1, left_i1 = matrix_entry(left, i, 1)
            right_r0, right_i0 = matrix_entry(right, 0, j)
            right_r1, right_i1 = matrix_entry(right, 1, j)
            pieces.append(
                left_r0 * right_r0 - left_i0 * right_i0 + left_r1 * right_r1 - left_i1 * right_i1
            )
            pieces.append(
                left_r0 * right_i0 + left_i0 * right_r0 + left_r1 * right_i1 + left_i1 * right_r1
            )
    return jnp.stack(pieces)


def adjoint(mat):
    return jnp.stack([mat[0], -mat[1], mat[4], -mat[5], mat[2], -mat[3], mat[6], -mat[7]])


def apply_gains(gain_p, coher_now, gain_q):
    return matmul_two(matmul_two(gain_p, coher_now), adjoint(gain_q))


def gram_parts(gram):
    return jnp.stack([gram[0], gram[6], gram[2], gram[3]])


def station_terms(gain_p, gain_q, coher_now, target):
    z_rows = matmul_two(coher_now, adjoint(gain_q))
    y_rows = matmul_two(adjoint(coher_now), adjoint(gain_p))
    leading_endpoint = jnp.concatenate(
        [matmul_two(target, adjoint(z_rows)), gram_parts(matmul_two(z_rows, adjoint(z_rows)))], 0
    )
    second = jnp.concatenate(
        [
            matmul_two(adjoint(target), adjoint(y_rows)),
            gram_parts(matmul_two(y_rows, adjoint(y_rows))),
        ],
        0,
    )
    return (jnp.sum(leading_endpoint, axis=1), jnp.sum(second, axis=1))


def solve_station(gathered_sums, gain_now, damp_value):
    numerator = gathered_sums[:8] + damp_value * gain_now
    diag_a = gathered_sums[8] + damp_value
    diag_d = gathered_sums[9] + damp_value
    cross_r = gathered_sums[10]
    cross_i = gathered_sums[11]
    determinant = diag_a * diag_d - cross_r * cross_r - cross_i * cross_i
    zeros_row = jnp.zeros_like(determinant)
    inverse = (
        jnp.stack([diag_d, zeros_row, -cross_r, -cross_i, -cross_r, cross_i, diag_a, zeros_row])
        / determinant
    )
    return matmul_two(numerator, inverse)


def on_device(visibilities, coherencies, gain_offsets, stations, solve_order, counts, damping):
    identity = jnp.zeros((8,), jnp.float32).at[0].set(1.0).at[6].set(1.0)
    start = lax.all_gather(gain_offsets, "bl", axis=2, tiled=True) + identity[None, :, None]
    groups = lax.axis_size("bl")
    channels = visibilities.shape[1]
    total_channels = coherencies.shape[2]
    owned_count = coherencies.shape[0]
    station_count = start.shape[2]
    damping_factor = visibilities.shape[2] * groups * total_channels / station_count
    lane_index = lax.axis_index("dir")
    ends_p = jnp.take(start, stations[0], axis=2)
    ends_q = jnp.take(start, stations[1], axis=2)
    owned_p = lax.dynamic_slice_in_dim(ends_p, lane_index * owned_count, owned_count, 0)
    owned_q = lax.dynamic_slice_in_dim(ends_q, lane_index * owned_count, owned_count, 0)
    gain_p = jnp.transpose(owned_p, (1, 0, 2))[:, :, None, :]
    gain_q = jnp.transpose(owned_q, (1, 0, 2))[:, :, None, :]
    coher_owned = jnp.transpose(coherencies, (1, 0, 2, 3)).astype(jnp.float32)
    partial_value = jnp.sum(apply_gains(gain_p, coher_owned, gain_q), axis=1)
    first_model = lax.psum_scatter(partial_value, "dir", scatter_dimension=1, tiled=True)
    first_residual = visibilities - first_model

    def direction_model(gain_now, coher_now):
        gain_p = jnp.take(gain_now, stations[0], axis=1)[:, None, :]
        gain_q = jnp.take(gain_now, stations[1], axis=1)[:, None, :]
        return apply_gains(gain_p, coher_now, gain_q)

    def sweep(step_index, state):
        gain_table, residual = state
        which = solve_order[step_index]
        owner_row = lax.dynamic_index_in_dim(coherencies, which % owned_count, 0, keepdims=False)
        broadcast_rows = from_root(owner_row, "dir", which // owned_count)
        coher_now = lax.dynamic_slice_in_dim(
            broadcast_rows, lane_index * channels, channels, 1
        ).astype(jnp.float32)
        damp_value = damping[which].astype(jnp.float32) * damping_factor
        gain_start = gain_table[which]
        target = residual + direction_model(gain_start, coher_now)

        def iterate(round_index, gain_now):
            gain_p = jnp.take(gain_now, stations[0], axis=1)[:, None, :]
            gain_q = jnp.take(gain_now, stations[1], axis=1)[:, None, :]
            leading_endpoint, second = station_terms(gain_p, gain_q, coher_now, target)
            local_sums = (
                jax.ops.segment_sum(leading_endpoint.T, stations[0], station_count)
                + jax.ops.segment_sum(second.T, stations[1], station_count)
            ).T
            gathered_sums = lax.psum(local_sums, ("bl", "dir"))
            updated = solve_station(gathered_sums, gain_now, damp_value)
            return jnp.where(round_index < counts[which], updated, gain_now)

        gain_final = lax.fori_loop(0, LM_ITERS, iterate, gain_start)
        residual = target - direction_model(gain_final, coher_now)
        return (gain_table.at[which].set(gain_final), residual)

    gain_table, residual = lax.fori_loop(0, SOLVED, sweep, (start, first_residual))
    own_width = station_count // groups
    gains = lax.dynamic_slice_in_dim(gain_table, lax.axis_index("bl") * own_width, own_width, 2)
    return (gains, residual)


def solution(mesh):
    return jax.shard_map(
        on_device,
        mesh=mesh,
        in_specs=(
            P(None, "dir", "bl"),
            P("dir", None, None, "bl"),
            P(None, None, "bl"),
            P(None, "bl"),
            P(),
            P(),
            P(),
        ),
        out_specs=(P(None, None, "bl"), P(None, "dir", "bl")),
        check_vma=False,
    )
```

profile of v0, /device:TPU:0, one launch (start us, length us, event | category | flops | bytes accessed | tf_op | source)
XLA Modules:
  0.0 740.6 jit_solution(11225464798927171772)
XLA Ops:
  9.1 16.8 %all_gather.3 = f32[32,8,512]{0,1,2:T(8,128)S(1)} all-gather(f32[32,8,64]{0,1,2:T(8,128)S(1)} %copy.381), channel_id=1, replica_groups=mesh['bl'=8,'dir'=4] {'bl'}, dimensions={2}, use_global_device_ids=true | all-gather | bytes 589824 | tf_op jit(solution)/shard_map/all_gather | solution.py:81
  29.4 2.0 gather_fusion.6
  31.4 1.6 select_bitcast_fusion.7
  34.7 1.6 copy.385
  36.3 1.6 copy.384
  37.9 1.6 copy.383
  39.4 1.6 copy.382
  44.0 1.6 copy.390
  46.3 1.6 subtract_dynamic-update-slice_fusion.1
  54.0 18.7 %reduce-scatter.2.cloned.1.call-done = f32[8,4,256]{2,0,1:T(8,128)} async-done(((f32[8,16,256]{2,0,1:T(8,128)}), f32[8,4,256]{2,0,1:T(8,128)}) %reduce-scatter.2.cloned.1.call-update) | async-done | bytes 32784 | tf_op jit(solution)/shard_map/reduce_scatter | solution.py:97
  73.5 659.7 %while.55 = (s32[]{:T(128)}, f32[32,8,512]{2,1,0:T(8,128)S(1)}, f32[8,4,256]{2,1,0:T(4,128)S(1)}, s32[32]{0:T(128)S(1)}, bf16[8,8,16,256]{3,2,1,0:T(8,128)(2,1)}...) while((s32[]{:T(128)}, f32[32,8,512]{2,1,0:T(8,128)S(1)}, ...), condition=%wide.region_12.15_spmd, body=%wide.region_2.14_spmd.sunk | while | flops 775727 | bytes 7942038 | solution.py:133
  85.4 25.5 %all-reduce.2.cloned.1.call-done = bf16[8,16,256]{2,1,0:T(8,128)(2,1)} async-done(((bf16[8,16,256]{2,1,0:T(8,128)(2,1)}), bf16[8,16,256]{2,1,0:T(8,128)(2,1)}) %all-reduce.2.cloned.1.call-update) | async-done | bytes 65552 | tf_op jit(solution)/shard_map/while/body/eval_jaxpr/psum | solution.py:12
  111.9 121.3 %while.56 = (s32[]{:T(128)}, f32[8,512]{0,1:T(8,128)S(1)}, s32[1]{0:T(128)}, s32[2,256]{1,0:T(2,128)S(1)}, f32[8,4,256]{2,1,0:T(4,128)S(1)}, /*index=5*/f32[8,4,...) while((s32[]{:T(128)}, f32[8,512]{0,1:T(8,128)S(1)}, ...), condition=%wide.region_11.13_spmd, body=%wide.region_5.12_spmd.sunk | while | flops 427009 | bytes 1846503 | solution.py:129
  115.4 1.5 scatter_custom_fusion.10
  117.2 1.5 scatter_custom_fusion.11
  118.7 42.9 %psum.30 = f32[12,512]{0,1:T(8,128)S(1)} all-reduce(f32[12,512]{0,1:T(8,128)S(1)} %add_bitcast_fusion.2), channel_id=1, replica_groups=mesh['bl'=8,'dir'=4] {'bl','dir'}, use_global_device_ids=true, to_apply=%region_10.11 | all-reduce | flops 6144 | bytes 49152 | tf_op jit(solution)/shard_map/while/body/eval_jaxpr/while/body/eval_jaxpr/psum | solution.py:125
  176.5 1.5 scatter_custom_fusion.10
  178.2 1.5 scatter_custom_fusion.11
  179.8 42.0 %psum.30 = f32[12,512]{0,1:T(8,128)S(1)} all-reduce(f32[12,512]{0,1:T(8,128)S(1)} %add_bitcast_fusion.2), channel_id=1, replica_groups=mesh['bl'=8,'dir'=4] {'bl','dir'}, use_global_device_ids=true, to_apply=%region_10.11 | all-reduce | flops 6144 | bytes 49152 | tf_op jit(solution)/shard_map/while/body/eval_jaxpr/while/body/eval_jaxpr/psum | solution.py:125
  249.7 26.2 %all-reduce.2.cloned.1.call-done = bf16[8,16,256]{2,1,0:T(8,128)(2,1)} async-done(((bf16[8,16,256]{2,1,0:T(8,128)(2,1)}), bf16[8,16,256]{2,1,0:T(8,128)(2,1)}) %all-reduce.2.cloned.1.call-update) | async-done | bytes 65552 | tf_op jit(solution)/shard_map/while/body/eval_jaxpr/psum | solution.py:12
  277.0 121.3 %while.56 = (s32[]{:T(128)}, f32[8,512]{0,1:T(8,128)S(1)}, s32[1]{0:T(128)}, s32[2,256]{1,0:T(2,128)S(1)}, f32[8,4,256]{2,1,0:T(4,128)S(1)}, /*index=5*/f32[8,4,...) while((s32[]{:T(128)}, f32[8,512]{0,1:T(8,128)S(1)}, ...), condition=%wide.region_11.13_spmd, body=%wide.region_5.12_spmd.sunk | while | flops 427009 | bytes 1846503 | solution.py:129
  280.5 1.5 scatter_custom_fusion.10
  283.8 42.9 %psum.30 = f32[12,512]{0,1:T(8,128)S(1)} all-reduce(f32[12,512]{0,1:T(8,128)S(1)} %add_bitcast_fusion.2), channel_id=1, replica_groups=mesh['bl'=8,'dir'=4] {'bl','dir'}, use_global_device_ids=true, to_apply=%region_10.11 | all-reduce | flops 6144 | bytes 49152 | tf_op jit(solution)/shard_map/while/body/eval_jaxpr/while/body/eval_jaxpr/psum | solution.py:125
  344.8 42.0 %psum.30 = f32[12,512]{0,1:T(8,128)S(1)} all-reduce(f32[12,512]{0,1:T(8,128)S(1)} %add_bitcast_fusion.2), channel_id=1, replica_groups=mesh['bl'=8,'dir'=4] {'bl','dir'}, use_global_device_ids=true, to_apply=%region_10.11 | all-reduce | flops 6144 | bytes 49152 | tf_op jit(solution)/shard_map/while/body/eval_jaxpr/while/body/eval_jaxpr/psum | solution.py:125
  414.8 26.2 %all-reduce.2.cloned.1.call-done = bf16[8,16,256]{2,1,0:T(8,128)(2,1)} async-done(((bf16[8,16,256]{2,1,0:T(8,128)(2,1)}), bf16[8,16,256]{2,1,0:T(8,128)(2,1)}) %all-reduce.2.cloned.1.call-update) | async-done | bytes 65552 | tf_op jit(solution)/shard_map/while/body/eval_jaxpr/psum | solution.py:12
  442.0 121.3 %while.56 = (s32[]{:T(128)}, f32[8,512]{0,1:T(8,128)S(1)}, s32[1]{0:T(128)}, s32[2,256]{1,0:T(2,128)S(1)}, f32[8,4,256]{2,1,0:T(4,128)S(1)}, /*index=5*/f32[8,4,...) while((s32[]{:T(128)}, f32[8,512]{0,1:T(8,128)S(1)}, ...), condition=%wide.region_11.13_spmd, body=%wide.region_5.12_spmd.sunk | while | flops 427009 | bytes 1846503 | solution.py:129
  448.8 42.9 %psum.30 = f32[12,512]{0,1:T(8,128)S(1)} all-reduce(f32[12,512]{0,1:T(8,128)S(1)} %add_bitcast_fusion.2), channel_id=1, replica_groups=mesh['bl'=8,'dir'=4] {'bl','dir'}, use_global_device_ids=true, to_apply=%region_10.11 | all-reduce | flops 6144 | bytes 49152 | tf_op jit(solution)/shard_map/while/body/eval_jaxpr/while/body/eval_jaxpr/psum | solution.py:125
  509.9 42.0 %psum.30 = f32[12,512]{0,1:T(8,128)S(1)} all-reduce(f32[12,512]{0,1:T(8,128)S(1)} %add_bitcast_fusion.2), channel_id=1, replica_groups=mesh['bl'=8,'dir'=4] {'bl','dir'}, use_global_device_ids=true, to_apply=%region_10.11 | all-reduce | flops 6144 | bytes 49152 | tf_op jit(solution)/shard_map/while/body/eval_jaxpr/while/body/eval_jaxpr/psum | solution.py:125
  579.9 26.2 %all-reduce.2.cloned.1.call-done = bf16[8,16,256]{2,1,0:T(8,128)(2,1)} async-done(((bf16[8,16,256]{2,1,0:T(8,128)(2,1)}), bf16[8,16,256]{2,1,0:T(8,128)(2,1)}) %all-reduce.2.cloned.1.call-update) | async-done | bytes 65552 | tf_op jit(solution)/shard_map/while/body/eval_jaxpr/psum | solution.py:12
  607.1 121.3 %while.56 = (s32[]{:T(128)}, f32[8,512]{0,1:T(8,128)S(1)}, s32[1]{0:T(128)}, s32[2,256]{1,0:T(2,128)S(1)}, f32[8,4,256]{2,1,0:T(4,128)S(1)}, /*index=5*/f32[8,4,...) while((s32[]{:T(128)}, f32[8,512]{0,1:T(8,128)S(1)}, ...), condition=%wide.region_11.13_spmd, body=%wide.region_5.12_spmd.sunk | while | flops 427009 | bytes 1846503 | solution.py:129
  613.9 42.9 %psum.30 = f32[12,512]{0,1:T(8,128)S(1)} all-reduce(f32[12,512]{0,1:T(8,128)S(1)} %add_bitcast_fusion.2), channel_id=1, replica_groups=mesh['bl'=8,'dir'=4] {'bl','dir'}, use_global_device_ids=true, to_apply=%region_10.11 | all-reduce | flops 6144 | bytes 49152 | tf_op jit(solution)/shard_map/while/body/eval_jaxpr/while/body/eval_jaxpr/psum | solution.py:125
  675.0 42.0 %psum.30 = f32[12,512]{0,1:T(8,128)S(1)} all-reduce(f32[12,512]{0,1:T(8,128)S(1)} %add_bitcast_fusion.2), channel_id=1, replica_groups=mesh['bl'=8,'dir'=4] {'bl','dir'}, use_global_device_ids=true, to_apply=%region_10.11 | all-reduce | flops 6144 | bytes 49152 | tf_op jit(solution)/shard_map/while/body/eval_jaxpr/while/body/eval_jaxpr/psum | solution.py:125
  (927 shorter events, 200.6 us)
Async XLA Ops:
  7.2 65.5 %reduce-scatter.2.cloned.1.call-start = ((), (), s32[]{:S(2)}) async-start(), calls=%async_computation.1 | async-start | bytes 163840 | tf_op jit(solution)/shard_map/reduce_scatter | solution.py:97
  50.9 22.6 %copy-start.21 = (s32[32]{0:T(128)S(1)}, s32[32]{0:T(128)}, u32[]{:S(2)}) copy-start(s32[32]{0:T(128)} %param.25) | copy-start | bytes 388
  50.9 22.6 %copy-start.23 = (s32[32]{0:T(128)S(1)}, s32[32]{0:T(128)}, u32[]{:S(2)}) copy-start(s32[32]{0:T(128)} %param.27) | copy-start | bytes 388
  50.9 22.6 %copy-start.25 = (s32[32]{0:T(128)S(1)}, s32[32]{0:T(128)}, u32[]{:S(2)}) copy-start(s32[32]{0:T(128)} %param.26) | copy-start | bytes 388
  73.7 38.0 %copy-start.5 = (f32[32,8,512]{2,1,0:T(8,128)}, f32[32,8,512]{2,1,0:T(8,128)S(1)}, u32[]{:S(2)}) copy-start(f32[32,8,512]{2,1,0:T(8,128)S(1)} %get-tuple-element.1500) | copy-start | bytes 1572868 | tf_op jit(solution)/shard_map/while
  73.7 37.1 %all-reduce.2.cloned.1.call-start = ((), (), s32[]{:S(2)}) async-start(), calls=%async_computation.2 | async-start | bytes 131072 | tf_op jit(solution)/shard_map/while/body/eval_jaxpr/psum | solution.py:12
  78.6 33.1 %copy-start.13 = (pred[256]{0:T(512)(128)(4,1)}, pred[256]{0:T(512)(128)(4,1)S(1)}, u32[]{:S(2)}) copy-start(pred[256]{0:T(512)(128)(4,1)S(1)} %get-tuple-element.1278) | copy-start | bytes 772 | tf_op jit(solution)/shard_map/while
  78.6 33.1 %copy-start.15 = (pred[256]{0:T(512)(128)(4,1)}, pred[256]{0:T(512)(128)(4,1)S(1)}, u32[]{:S(2)}) copy-start(pred[256]{0:T(512)(128)(4,1)S(1)} %get-tuple-element.1272) | copy-start | bytes 772 | tf_op jit(solution)/shard_map/while
  80.0 31.8 %copy-start.1 = (f32[1,8,512]{1,2,0:T(8,128)}, f32[1,8,512]{1,2,0:T(8,128)S(1)}, u32[]{:S(2)}) copy-start(f32[1,8,512]{1,2,0:T(8,128)S(1)} %copy.423) | copy-start | bytes 49156 | tf_op jit(solution)/shard_map/while
  82.1 29.5 %copy-start.8 = (s32[1024]{0:T(1024)}, s32[1024]{0:T(1024)S(1)}, u32[]{:S(2)}) copy-start(s32[1024]{0:T(1024)S(1)} %pad_clamp_fusion.10) | copy-start | bytes 12292 | tf_op jit(solution)/shard_map/while
  111.9 124.4 %copy-start.16 = (pred[256]{0:T(512)(128)(4,1)S(1)}, pred[256]{0:T(512)(128)(4,1)}, u32[]{:S(2)}) copy-start(pred[256]{0:T(512)(128)(4,1)} %copy-done.15) | copy-start | bytes 772 | tf_op jit(solution)/shard_map/while
  238.0 38.8 %copy-start.5 = (f32[32,8,512]{2,1,0:T(8,128)}, f32[32,8,512]{2,1,0:T(8,128)S(1)}, u32[]{:S(2)}) copy-start(f32[32,8,512]{2,1,0:T(8,128)S(1)} %get-tuple-element.1500) | copy-start | bytes 1572868 | tf_op jit(solution)/shard_map/while
  238.1 37.9 %all-reduce.2.cloned.1.call-start = ((), (), s32[]{:S(2)}) async-start(), calls=%async_computation.2 | async-start | bytes 131072 | tf_op jit(solution)/shard_map/while/body/eval_jaxpr/psum | solution.py:12
  242.9 33.8 %copy-start.13 = (pred[256]{0:T(512)(128)(4,1)}, pred[256]{0:T(512)(128)(4,1)S(1)}, u32[]{:S(2)}) copy-start(pred[256]{0:T(512)(128)(4,1)S(1)} %get-tuple-element.1278) | copy-start | bytes 772 | tf_op jit(solution)/shard_map/while
  242.9 33.8 %copy-start.15 = (pred[256]{0:T(512)(128)(4,1)}, pred[256]{0:T(512)(128)(4,1)S(1)}, u32[]{:S(2)}) copy-start(pred[256]{0:T(512)(128)(4,1)S(1)} %get-tuple-element.1272) | copy-start | bytes 772 | tf_op jit(solution)/shard_map/while
  244.4 32.6 %copy-start.1 = (f32[1,8,512]{1,2,0:T(8,128)}, f32[1,8,512]{1,2,0:T(8,128)S(1)}, u32[]{:S(2)}) copy-start(f32[1,8,512]{1,2,0:T(8,128)S(1)} %copy.423) | copy-start | bytes 49156 | tf_op jit(solution)/shard_map/while
  246.5 30.2 %copy-start.8 = (s32[1024]{0:T(1024)}, s32[1024]{0:T(1024)S(1)}, u32[]{:S(2)}) copy-start(s32[1024]{0:T(1024)S(1)} %pad_clamp_fusion.10) | copy-start | bytes 12292 | tf_op jit(solution)/shard_map/while
  277.0 124.4 %copy-start.16 = (pred[256]{0:T(512)(128)(4,1)S(1)}, pred[256]{0:T(512)(128)(4,1)}, u32[]{:S(2)}) copy-start(pred[256]{0:T(512)(128)(4,1)} %copy-done.15) | copy-start | bytes 772 | tf_op jit(solution)/shard_map/while
  403.1 38.8 %copy-start.5 = (f32[32,8,512]{2,1,0:T(8,128)}, f32[32,8,512]{2,1,0:T(8,128)S(1)}, u32[]{:S(2)}) copy-start(f32[32,8,512]{2,1,0:T(8,128)S(1)} %get-tuple-element.1500) | copy-start | bytes 1572868 | tf_op jit(solution)/shard_map/while
  403.1 37.9 %all-reduce.2.cloned.1.call-start = ((), (), s32[]{:S(2)}) async-start(), calls=%async_computation.2 | async-start | bytes 131072 | tf_op jit(solution)/shard_map/while/body/eval_jaxpr/psum | solution.py:12
  408.0 33.8 %copy-start.13 = (pred[256]{0:T(512)(128)(4,1)}, pred[256]{0:T(512)(128)(4,1)S(1)}, u32[]{:S(2)}) copy-start(pred[256]{0:T(512)(128)(4,1)S(1)} %get-tuple-element.1278) | copy-start | bytes 772 | tf_op jit(solution)/shard_map/while
  408.0 33.8 %copy-start.15 = (pred[256]{0:T(512)(128)(4,1)}, pred[256]{0:T(512)(128)(4,1)S(1)}, u32[]{:S(2)}) copy-start(pred[256]{0:T(512)(128)(4,1)S(1)} %get-tuple-element.1272) | copy-start | bytes 772 | tf_op jit(solution)/shard_map/while
  409.4 32.6 %copy-start.1 = (f32[1,8,512]{1,2,0:T(8,128)}, f32[1,8,512]{1,2,0:T(8,128)S(1)}, u32[]{:S(2)}) copy-start(f32[1,8,512]{1,2,0:T(8,128)S(1)} %copy.423) | copy-start | bytes 49156 | tf_op jit(solution)/shard_map/while
  411.5 30.2 %copy-start.8 = (s32[1024]{0:T(1024)}, s32[1024]{0:T(1024)S(1)}, u32[]{:S(2)}) copy-start(s32[1024]{0:T(1024)S(1)} %pad_clamp_fusion.10) | copy-start | bytes 12292 | tf_op jit(solution)/shard_map/while
  442.0 124.4 %copy-start.16 = (pred[256]{0:T(512)(128)(4,1)S(1)}, pred[256]{0:T(512)(128)(4,1)}, u32[]{:S(2)}) copy-start(pred[256]{0:T(512)(128)(4,1)} %copy-done.15) | copy-start | bytes 772 | tf_op jit(solution)/shard_map/while
  568.2 38.8 %copy-start.5 = (f32[32,8,512]{2,1,0:T(8,128)}, f32[32,8,512]{2,1,0:T(8,128)S(1)}, u32[]{:S(2)}) copy-start(f32[32,8,512]{2,1,0:T(8,128)S(1)} %get-tuple-element.1500) | copy-start | bytes 1572868 | tf_op jit(solution)/shard_map/while
  568.2 37.9 %all-reduce.2.cloned.1.call-start = ((), (), s32[]{:S(2)}) async-start(), calls=%async_computation.2 | async-start | bytes 131072 | tf_op jit(solution)/shard_map/while/body/eval_jaxpr/psum | solution.py:12
  573.0 33.8 %copy-start.13 = (pred[256]{0:T(512)(128)(4,1)}, pred[256]{0:T(512)(128)(4,1)S(1)}, u32[]{:S(2)}) copy-start(pred[256]{0:T(512)(128)(4,1)S(1)} %get-tuple-element.1278) | copy-start | bytes 772 | tf_op jit(solution)/shard_map/while
  573.0 33.8 %copy-start.15 = (pred[256]{0:T(512)(128)(4,1)}, pred[256]{0:T(512)(128)(4,1)S(1)}, u32[]{:S(2)}) copy-start(pred[256]{0:T(512)(128)(4,1)S(1)} %get-tuple-element.1272) | copy-start | bytes 772 | tf_op jit(solution)/shard_map/while
  574.5 32.6 %copy-start.1 = (f32[1,8,512]{1,2,0:T(8,128)}, f32[1,8,512]{1,2,0:T(8,128)S(1)}, u32[]{:S(2)}) copy-start(f32[1,8,512]{1,2,0:T(8,128)S(1)} %copy.423) | copy-start | bytes 49156 | tf_op jit(solution)/shard_map/while
  576.6 30.2 %copy-start.8 = (s32[1024]{0:T(1024)}, s32[1024]{0:T(1024)S(1)}, u32[]{:S(2)}) copy-start(s32[1024]{0:T(1024)S(1)} %pad_clamp_fusion.10) | copy-start | bytes 12292 | tf_op jit(solution)/shard_map/while
  607.1 124.4 %copy-start.16 = (pred[256]{0:T(512)(128)(4,1)S(1)}, pred[256]{0:T(512)(128)(4,1)}, u32[]{:S(2)}) copy-start(pred[256]{0:T(512)(128)(4,1)} %copy-done.15) | copy-start | bytes 772 | tf_op jit(solution)/shard_map/while
  (46 other events, 191.0 us)
Sparse Core Ops, SparseCore 0:
  53.2 19.4 reduce-scatter.1
  78.6 32.1 all-reduce.1
  243.0 32.9 all-reduce.1
  408.0 32.9 all-reduce.1
  573.1 32.9 all-reduce.1
where the time goes:
time: 744 us; the launch traced here: 741 us
  blocking collectives  356 us (48%)
  local copies, waits for them, and re-layouts  134 us (18%)
  waiting for transfers between devices  123 us (17%)
  other arithmetic  86.8 us (12%)
  loops' own time  26.5 us (4%)
  between operations  13.9 us (2%)
    psum x8, blocking collectives, iterate(): gathered_sums = lax.psum(local_sums, ('bl', 'dir'))  340 us
    psum x4, waiting for transfers between devices, from_root(): return lax.psum(jnp.where(mine, shard, jnp.zeros_like(shard)), axis)  104 us
    slice x161, local copies, waits for them, and re-layouts, matrix_entry(): return (mat[4 * i + 2 * j], mat[4 * i + 2 * j + 1])  74.1 us
    another operation x1, loops' own time, on_device(): lax.fori_loop(0, SOLVED, sweep, (start, first_residual))  19.6 us
    reduce_scatter x1, waiting for transfers between devices, on_device(): lax.psum_scatter(partial_value, 'dir', scatter_dimension=1, tiled=True)  18.7 us
    all_gather x1, blocking collectives, on_device(): lax.all_gather(gain_offsets, 'bl', axis=2, tiled=True)  16.8 us
  transfers between devices with their start and end apart: 5, of which 5 were waited for; matrix products, arithmetic and copies ran while one was open for 3% of the time, Pallas kernels for 0%

commit v1 on v0

v1 whole, which is shorter than its diff:
```python
import functools

import jax
import jax.numpy as jnp
from jax import lax
from jax.experimental import pallas as pl
from jax.experimental.pallas import tpu as pltpu
from jax.sharding import PartitionSpec as P

LM_ITERS = 2
SOLVED = 4
F32 = jnp.float32
BF16 = jnp.bfloat16
VMEM_BYTES = 48 * 1024 * 1024
PAIRS = [(m, i) for i in range(SOLVED) for m in range(i)]
GRAM = [(u, v) for u in range(4) for v in range(u, 4)]
M_ROWS = 32
K_ROWS = 16
KX_ROWS = SOLVED * K_ROWS + len(PAIRS) * M_ROWS + 8
ALL_ROWS = SOLVED * M_ROWS + KX_ROWS
STATION_ROW = ALL_ROWS - 8


def mul(x, y):
    return (x[0] * y[0] - x[1] * y[1], x[0] * y[1] + x[1] * y[0])


def add(x, y):
    return (x[0] + y[0], x[1] + y[1])


def sub(x, y):
    return (x[0] - y[0], x[1] - y[1])


def conj(x):
    return (x[0], -x[1])


def total(terms):
    return functools.reduce(add, terms)


def mul_conj(x, y):
    return (x[0] * y[0] + x[1] * y[1], x[1] * y[0] - x[0] * y[1])


def matmul(left, right):
    return [add(mul(left[2 * i], right[j]), mul(left[2 * i + 1], right[2 + j])) for i in (0, 1) for j in (0, 1)]


def matmul_adj(left, right):
    return [
        add(mul_conj(left[2 * i], right[2 * j]), mul_conj(left[2 * i + 1], right[2 * j + 1]))
        for i in (0, 1)
        for j in (0, 1)
    ]


def apply_gains(gain_p, coher, gain_q):
    return matmul_adj(matmul(gain_p, coher), gain_q)


def as_matrix(parts):
    return [(parts[2 * e], parts[2 * e + 1]) for e in range(4)]


def split_rows(values):
    high = values.astype(BF16)
    low = (values - high.astype(F32)).astype(BF16)
    return jnp.concatenate([high, low], axis=0)


def one_hot(stations_p, stations_q, count):
    both = jnp.concatenate([stations_p, stations_q], axis=1)
    rows = lax.broadcasted_iota(jnp.int32, (count, both.shape[1]), 0)
    return jnp.where(rows == both, 1.0, 0.0).astype(BF16)


def pick(one_hots, values):
    count = values.shape[0]
    out = jnp.dot(split_rows(values), one_hots, preferred_element_type=F32)
    return out[:count] + out[count:]


def prep_kernel(place_ref, offs_ref, out_ref, *, owned, per):
    width = offs_ref.shape[2]
    part_rows = out_ref.shape[0]
    comp = lax.broadcasted_iota(jnp.int32, (8, width), 0)
    ident = jnp.where((comp == 0) | (comp == 6), 1.0, 0.0)
    blocks = [offs_ref[place_ref[d]] + ident for d in range(owned + SOLVED)]
    while len(blocks) * 8 < part_rows * per:
        blocks.append(jnp.zeros((8, width), F32))
    each = part_rows // 8
    columns = [jnp.concatenate(blocks[q * each : (q + 1) * each], axis=0) for q in range(per)]
    out_ref[...] = jnp.concatenate(columns, axis=1)


def model_kernel(
    base_ref, flag_ref, blocks_ref, stations_ref, coher_ref, solved_ref, vis_ref, part_ref, m_ref, kx_ref, start_ref, table, ends,
    *, width
):
    owned = coher_ref.shape[0]
    baselines = coher_ref.shape[3]
    groups, part_rows, lanes = blocks_ref.shape
    per = lanes // width
    count = groups * width
    lane_of = lax.broadcasted_iota(jnp.int32, (part_rows, lanes), 1) // width
    for tile in range(count // lanes):
        for q in range(per):
            tile_rows = jnp.zeros((part_rows, lanes), F32)
            for u in range(per):
                block = blocks_ref[per * tile + u]
                shift = ((u - q) * width) % lanes
                if shift:
                    block = pltpu.roll(block, shift, 1)
                tile_rows = jnp.where(lane_of == u, block, tile_rows)
            table[q * part_rows : (q + 1) * part_rows, tile * lanes : (tile + 1) * lanes] = tile_rows
    start_ref[...] = table[owned * 8 : (owned + SOLVED) * 8, :]
    local = stations_ref[...] ^ base_ref[0]
    ends[...] = pick(one_hot(local[0:1], local[1:2], count), table[...])
    for half in range(baselines // 128):
        kx_ref[half, KX_ROWS - 8 : KX_ROWS, :] = jnp.zeros((8, 128), F32)
        kx_ref[half, KX_ROWS - 8 : KX_ROWS - 6, :] = stations_ref[:, half * 128 : half * 128 + 128].astype(F32)

    def summed(values):
        return jnp.sum(values, axis=0, keepdims=True)

    for half in range(baselines // 128):
        at = pl.ds(half * 128, 128)
        at_q = pl.ds(baselines + half * 128, 128)

        def gain(row, where):
            block = ends[pl.ds(pl.multiple_of(row, 8), 8), where]
            return as_matrix([block[c : c + 1] for c in range(8)])

        def add_model(d, acc):
            coher = as_matrix([coher_ref[d, c, :, at].astype(F32) for c in range(8)])
            model = apply_gains(gain(d * 8, at), coher, gain(d * 8, at_q))
            return [sub(x, y) for x, y in zip(acc, model)]

        acc = as_matrix([vis_ref[c, :, at] for c in range(8)])
        acc = lax.fori_loop(0, owned, add_model, acc)
        for e in range(4):
            part_ref[2 * e, :, at] = acc[e][0]
            part_ref[2 * e + 1, :, at] = acc[e][1]
        for i in range(SOLVED):
            coher = as_matrix([solved_ref[i, c, :, at].astype(F32) for c in range(8)])
            row = (owned + i) * 8
            model = apply_gains(gain(row, at), coher, gain(row, at_q))
            flag = flag_ref[i]
            target = [
                (part_ref[2 * e, :, at] + flag * model[e][0], part_ref[2 * e + 1, :, at] + flag * model[e][1])
                for e in range(4)
            ]
            for u in range(4):
                for v in range(4):
                    value = mul_conj(target[u], coher[v])
                    out = i * M_ROWS + (u * 4 + v) * 2
                    m_ref[half, out : out + 1, :] = summed(value[0])
                    m_ref[half, out + 1 : out + 2, :] = summed(value[1])
            out = i * K_ROWS
            for u, v in GRAM:
                value = mul_conj(coher[u], coher[v])
                kx_ref[half, out : out + 1, :] = summed(value[0])
                out += 1
                if u != v:
                    kx_ref[half, out : out + 1, :] = summed(value[1])
                    out += 1
            for m in range(i):
                other = as_matrix([solved_ref[m, c, :, at].astype(F32) for c in range(8)])
                out = SOLVED * K_ROWS + PAIRS.index((m, i)) * M_ROWS
                for u in range(4):
                    for v in range(4):
                        value = mul_conj(other[u], coher[v])
                        kx_ref[half, out : out + 1, :] = summed(value[0])
                        kx_ref[half, out + 1 : out + 2, :] = summed(value[1])
                        out += 2


def sweep_kernel(
    base_ref, which_ref, rounds_ref, damp_ref, sums_ref, start_ref, offs_ref, first_ref, own_ref, gains_ref, out_ref,
    hots, ends, values, state, m_now, k_now, moved,
    *, groups
):
    count = start_ref.shape[1]
    baselines = first_ref.shape[2]
    width = offs_ref.shape[2]
    stride = ALL_ROWS
    tiles = baselines // 128
    chunks = groups * tiles

    comp = lax.broadcasted_iota(jnp.int32, (8, width), 0)
    gains_ref[...] = offs_ref[...] + jnp.where((comp == 0) | (comp == 6), 1.0, 0.0)[None]
    values[...] = jnp.zeros(values.shape, F32)
    for g in range(groups):
        starts = [(g * tiles + t) * stride + STATION_ROW for t in range(tiles)]
        rows = jnp.concatenate([sums_ref[at : at + 8, :] for at in starts], axis=1).astype(jnp.int32) ^ base_ref[0]
        hots[g] = one_hot(rows[0:1], rows[1:2], count)

    def rows_at(row):
        return sums_ref[pl.ds(row, chunks, stride=stride), :]

    def fetch(gain_now, slot):
        split = split_rows(gain_now)
        for g in range(groups):
            out = jnp.dot(split, hots[g], preferred_element_type=F32)
            out = out[:8] + out[8:]
            for end in (0, 1):
                for t in range(tiles):
                    chunk, column = (g * tiles + t) * 8, (end * tiles + t) * 128
                    ends[slot, end, chunk : chunk + 8, :] = out[:, column : column + 128]

    def gain_at(slot):
        return [as_matrix([ends[slot, end, pl.ds(c, chunks, stride=8), :] for c in range(8)]) for end in (0, 1)]

    def load_m():
        return [[(m_now[(u * 4 + v) * 2], m_now[(u * 4 + v) * 2 + 1]) for v in range(4)] for u in range(4)]

    def load_k():
        row = 0
        gram = {}
        for u, v in GRAM:
            if u == v:
                gram[u, v] = (k_now[row], None)
                row += 1
            else:
                gram[u, v] = (k_now[row], k_now[row + 1])
                gram[v, u] = conj(gram[u, v])
                row += 2
        return gram

    def prepare(i):
        for row in range(K_ROWS):
            k_now[row] = rows_at(SOLVED * M_ROWS + i * K_ROWS + row)
        for out in range(4):
            for w in range(4):
                row = (out * 4 + w) * 2
                value = (rows_at(i * M_ROWS + row), rows_at(i * M_ROWS + row + 1))
                for m in range(i):
                    base = SOLVED * M_ROWS + SOLVED * K_ROWS + PAIRS.index((m, i)) * M_ROWS
                    for uv in range(4):
                        delta = (moved[m, (out * 4 + uv) * 2], moved[m, (out * 4 + uv) * 2 + 1])
                        at = base + (uv * 4 + w) * 2
                        value = add(value, mul(delta, (rows_at(at), rows_at(at + 1))))
                m_now[row] = value[0]
                m_now[row + 1] = value[1]

    def hermitian(gain):
        a = gain[0][0] ** 2 + gain[0][1] ** 2 + gain[2][0] ** 2 + gain[2][1] ** 2
        d = gain[1][0] ** 2 + gain[1][1] ** 2 + gain[3][0] ** 2 + gain[3][1] ** 2
        cross = add(mul_conj(gain[1], gain[0]), mul_conj(gain[3], gain[2]))
        return a, d, cross

    def normal_terms(slot):
        gain_p, gain_q = gain_at(slot)
        m = load_m()
        k = load_k()
        for end, gain, other in ((0, gain_q, False), (1, gain_p, True)):
            row = 0
            for r in (0, 1):
                for c in (0, 1):
                    if other:
                        terms = [mul_conj(gain[2 * a + b], m[2 * a + r][2 * b + c]) for a in (0, 1) for b in (0, 1)]
                    else:
                        terms = [mul(gain[2 * a + b], m[2 * r + a][2 * c + b]) for a in (0, 1) for b in (0, 1)]
                    value = total(terms)
                    values[end, pl.ds(row, chunks, stride=16), :] = value[0]
                    values[end, pl.ds(row + 1, chunks, stride=16), :] = value[1]
                    row += 2
            a, d, cross = hermitian(gain)
            for r, c in ((0, 0), (1, 1), (0, 1)):
                if other:
                    kk = [[k[2 * x + r, 2 * y + c] for y in (0, 1)] for x in (0, 1)]
                    kk = [[(z[0], None if z[1] is None else -z[1]) for z in line] for line in kk]
                else:
                    kk = [[k[2 * r + x, 2 * c + y] for y in (0, 1)] for x in (0, 1)]
                real = a * kk[0][0][0] + d * kk[1][1][0]
                real += cross[0] * (kk[0][1][0] + kk[1][0][0])
                minus = None
                if kk[0][1][1] is not None:
                    minus = kk[1][0][1] - kk[0][1][1]
                    real += cross[1] * minus
                values[end, pl.ds(row, chunks, stride=16), :] = real
                row += 1
                if r != c:
                    imag = cross[1] * (kk[0][1][0] - kk[1][0][0])
                    if kk[0][0][1] is not None:
                        imag += a * kk[0][0][1]
                    if kk[1][1][1] is not None:
                        imag += d * kk[1][1][1]
                    if kk[0][1][1] is not None:
                        imag += cross[0] * kk[0][1][1]
                    if kk[1][0][1] is not None:
                        imag += cross[0] * kk[1][0][1]
                    values[end, pl.ds(row, chunks, stride=16), :] = imag
                    row += 1

    def station_sums():
        acc = jnp.zeros((32, count), F32)
        for g in range(groups):
            starts = [(end, (g * tiles + t) * 16) for end in (0, 1) for t in range(tiles)]
            split = split_rows(jnp.concatenate([values[end, at : at + 16, :] for end, at in starts], axis=1))
            acc += lax.dot_general(split, hots[g], (((1,), (1,)), ((), ())), preferred_element_type=F32)
        return acc[:16] + acc[16:]

    def solve(sums, gain_now, damp):
        numer = sums[:8] + damp * gain_now
        numer = as_matrix([numer[c : c + 1] for c in range(8)])
        diag_a = sums[8:9] + damp
        diag_d = sums[9:10] + damp
        cross_r = sums[10:11]
        cross_i = sums[11:12]
        scale = 1.0 / (diag_a * diag_d - cross_r * cross_r - cross_i * cross_i)
        rows = []
        for r in (0, 1):
            x, y = numer[2 * r], numer[2 * r + 1]
            low = mul(y, (cross_r, -cross_i))
            high = mul(x, (cross_r, cross_i))
            rows += [x[0] * diag_d - low[0], x[1] * diag_d - low[1]]
            rows += [y[0] * diag_a - high[0], y[1] * diag_a - high[1]]
        return jnp.concatenate([value * scale for value in rows], axis=0)

    out_ref[...] = first_ref[...]
    for i in range(SOLVED):
        begin = start_ref[i * 8 : i * 8 + 8, :]
        damp = damp_ref[i]
        state[...] = begin
        fetch(begin, 0)
        prepare(i)

        def round_body(r, slot):
            normal_terms(slot)
            updated = solve(station_sums(), state[...], damp)
            state[...] = updated
            fetch(updated, 1)
            return jnp.int32(1)

        lax.fori_loop(0, rounds_ref[i], round_body, jnp.int32(0))
        gains_ref[which_ref[i]] = state[:, :width]

        for tile in range(tiles):
            at = pl.ds(tile * 128, 128)
            coher = as_matrix([own_ref[i, c, :, at].astype(F32) for c in range(8)])
            own = [
                [as_matrix([ends[slot, end, tile * 8 + c : tile * 8 + c + 1, :] for c in range(8)]) for end in (0, 1)]
                for slot in (0, 1)
            ]
            before = apply_gains(own[0][0], coher, own[0][1])
            after = apply_gains(own[1][0], coher, own[1][1])
            for e in range(4):
                change = sub(before[e], after[e])
                out_ref[2 * e, :, at] += change[0]
                out_ref[2 * e + 1, :, at] += change[1]
        if i + 1 == SOLVED:
            break
        p0, q0 = gain_at(0)
        p1, q1 = gain_at(1)
        for a in (0, 1):
            for b in (0, 1):
                for u in (0, 1):
                    for v in (0, 1):
                        delta = sub(mul_conj(p0[2 * a + u], q0[2 * b + v]), mul_conj(p1[2 * a + u], q1[2 * b + v]))
                        row = ((2 * a + b) * 4 + 2 * u + v) * 2
                        moved[i, row] = delta[0]
                        moved[i, row + 1] = delta[1]


def vmem():
    return pl.BlockSpec(memory_space=pltpu.VMEM)


def smem():
    return pl.BlockSpec(memory_space=pltpu.SMEM)


def exchange(block, axis, mask):
    return lax.ppermute(block, axis, [(i, i ^ mask) for i in range(lax.axis_size(axis))])


def butterfly_sum(value, axis):
    mask = 1
    while mask < lax.axis_size(axis):
        value = value + exchange(value, axis, mask)
        mask *= 2
    return value


def gather_blocks(block, axis):
    parts = block[None]
    size = lax.axis_size(axis)
    masks = [1 << s for s in range(size.bit_length() - 1)]
    for mask in masks[1:]:
        parts = jnp.concatenate([parts, exchange(parts, axis, mask)], axis=0)
    parts = jnp.stack([parts, exchange(parts, axis, masks[0])], axis=1)
    return parts.reshape((size,) + block.shape)


def on_device(visibilities, coherencies, gain_offsets, stations, solve_order, counts, damping):
    groups = lax.axis_size("bl")
    lane, own = lax.axis_index("dir"), lax.axis_index("bl")
    owned, _, channel_count, baselines = coherencies.shape
    channels = visibilities.shape[1]
    width = gain_offsets.shape[2]
    count = groups * width
    solved = solve_order[:SOLVED]
    rounds = jnp.minimum(counts[solved], LM_ITERS)
    damp = damping[solved].astype(F32) * (baselines * groups * channel_count / count)
    mine = (solved // owned) == lane
    base = (own * width).astype(jnp.int32)[None]

    per = 128 // width
    part_rows = -(-(owned + SOLVED) // per) * 8
    places = jnp.concatenate([lane * owned + jnp.arange(owned, dtype=jnp.int32), solved])
    params = pltpu.CompilerParams(vmem_limit_bytes=VMEM_BYTES)
    packed = pl.pallas_call(
        functools.partial(prep_kernel, owned=owned, per=per),
        out_shape=jax.ShapeDtypeStruct((part_rows, 128), F32),
        in_specs=[smem(), vmem()],
        out_specs=vmem(),
        compiler_params=params,
        name="pack_gains",
    )(places, gain_offsets)
    blocks = gather_blocks(packed, "bl")

    chosen = jnp.stack(
        [
            jnp.where(mine[i], lax.dynamic_index_in_dim(coherencies, solved[i] % owned, 0, keepdims=False), 0)
            for i in range(SOLVED)
        ]
    ).astype(BF16)
    shared = butterfly_sum(chosen, "dir")
    own_channels = lax.dynamic_slice_in_dim(shared, lane * channels, channels, 2)
    vis = lax.dynamic_update_slice_in_dim(
        jnp.zeros((8, channel_count, baselines), F32), visibilities, lane * channels, 1
    )

    part, m_part, kx, start = pl.pallas_call(
        functools.partial(model_kernel, width=width),
        out_shape=(
            jax.ShapeDtypeStruct((8, channel_count, baselines), F32),
            jax.ShapeDtypeStruct((baselines // 128, SOLVED * M_ROWS, 128), F32),
            jax.ShapeDtypeStruct((baselines // 128, KX_ROWS, 128), F32),
            jax.ShapeDtypeStruct((SOLVED * 8, count), F32),
        ),
        in_specs=[smem()] * 2 + [vmem()] * 5,
        out_specs=(vmem(),) * 4,
        scratch_shapes=[pltpu.VMEM((part_rows * per, count), F32), pltpu.VMEM((part_rows * per, 2 * baselines), F32)],
        compiler_params=params,
        name="first_model",
    )(base, mine.astype(F32), blocks, stations, coherencies, shared, vis)

    first = lax.psum_scatter(part, "dir", scatter_dimension=1, tiled=True)
    sums = jnp.concatenate([butterfly_sum(m_part, "dir"), kx], axis=1)
    everything = gather_blocks(sums, "bl").reshape(-1, 128)

    gains, residual = pl.pallas_call(
        functools.partial(sweep_kernel, groups=groups),
        out_shape=(
            jax.ShapeDtypeStruct(gain_offsets.shape, F32),
            jax.ShapeDtypeStruct(visibilities.shape, F32),
        ),
        in_specs=[smem()] * 4 + [vmem()] * 5,
        out_specs=(vmem(), vmem()),
        scratch_shapes=[
            pltpu.VMEM((groups, count, 2 * baselines), BF16),
            pltpu.VMEM((2, 2, groups * baselines // 16, 128), F32),
            pltpu.VMEM((2, groups * baselines // 8, 128), F32),
            pltpu.VMEM((8, count), F32),
            pltpu.VMEM((M_ROWS, groups * baselines // 128, 128), F32),
            pltpu.VMEM((K_ROWS, groups * baselines // 128, 128), F32),
            pltpu.VMEM((SOLVED - 1, M_ROWS, groups * baselines // 128, 128), F32),
        ],
        compiler_params=params,
        name="sweep",
    )(base, solved, rounds, damp, everything, start, gain_offsets, first, own_channels)
    return gains, residual


def solution(mesh):
    return jax.shard_map(
        on_device,
        mesh=mesh,
        in_specs=(
            P(None, "dir", "bl"),
            P("dir", None, None, "bl"),
            P(None, None, "bl"),
            P(None, "bl"),
            P(),
            P(),
            P(),
        ),
        out_specs=(P(None, None, "bl"), P(None, "dir", "bl")),
        check_vma=False,
    )
```

time: 744 us -> 146 us (0.20)
  blocking collectives: 356 us -> 0 us
  local copies, waits for them, and re-layouts: 134 us -> 6.86 us
  other arithmetic: 86.8 us -> 8.24 us
  waiting for transfers between devices: 123 us -> 70.7 us
  loops' own time: 26.5 us -> 0 us
  Pallas kernels: 0 us -> 22.8 us
  starting transfers between devices: 0.21 us -> 14.8 us
  between operations: 13.9 us -> 22 us
    psum x8 -> x0, blocking collectives: 340 us -> none  [iterate(): gathered_sums = lax.psum(local_sums, ('bl', 'dir'))]
    psum x4 -> x0, waiting for transfers between devices: 104 us -> none  [from_root(): return lax.psum(jnp.where(mine, shard, jnp.zeros_like(shard)), axis)]
    slice x174 -> x2, local copies, waits for them, and re-layouts: 74.9 us -> 2.16 us  [the longest x1 1.48 us: on_device(): solved[i] % owned]
    ppermute x0 -> x10, waiting for transfers between devices: none -> 48.2 us  [exchange(): lax.ppermute(block, axis, [(i, i ^ mask) for i in range(lax.axis_size(axi...]
    gather x35 -> x2, local copies, waits for them, and re-layouts: 27.9 us -> 1.28 us  [the longest x1 0.64 us: on_device(): rounds = jnp.minimum(counts[solved], LM_ITERS)]
    another operation x5 -> x0, loops' own time: 26.5 us -> none  [the longest x1 19.6 us: on_device(): lax.fori_loop(0, SOLVED, sweep, (start, first_residual))]
    scatter-add x16 -> x0, other arithmetic: 23.8 us -> none  [the longest x8 11.9 us: iterate(): jax.ops.segment_sum(leading_endpoint.T, stations[0], station_count)]
    pallas_call x0 -> x3, Pallas kernels: none -> 22.8 us  [the longest x1 19.1 us: on_device(): pl.pallas_call(functools.partial(sweep_kernel, groups=groups), out_shape=...]
  transfers between devices with their start and end apart: 5 -> 11, of which waited for: 5 -> 8; matrix products, arithmetic and copies ran while one was open for 3% -> 3% of each run, Pallas kernels for 0% -> 0%
where the time goes in v1:
time: 146 us; the launch traced here: 145 us
  waiting for transfers between devices  70.7 us (48%)
  Pallas kernels  22.8 us (16%)
  between operations  22 us (15%)
  starting transfers between devices  14.8 us (10%)
  other arithmetic  8.24 us (6%)
  local copies, waits for them, and re-layouts  6.86 us (5%)
    ppermute x10, waiting for transfers between devices, exchange(): lax.ppermute(block, axis, [(i, i ^ mask) for i in range(lax.axis_size(axi...  48.2 us
    reduce_scatter x1, waiting for transfers between devices, on_device(): first = lax.psum_scatter(part, 'dir', scatter_dimension=1, tiled=True)  22.5 us
    pallas_call x1, Pallas kernels, on_device(): pl.pallas_call(functools.partial(sweep_kernel, groups=groups), out_shape=...  19.1 us
    ppermute x10, starting transfers between devices, exchange(): lax.ppermute(block, axis, [(i, i ^ mask) for i in range(lax.axis_size(axi...  14.8 us
    select_n x1, other arithmetic, on_device(): jnp.where(mine[i], lax.dynamic_index_in_dim(coherencies, solved[i] % owne...  3.51 us
    pallas_call x1, Pallas kernels, on_device(): pl.pallas_call(functools.partial(model_kernel, width=width), out_shape=(j...  3.15 us
    another operation x4, other arithmetic, gather_blocks(): parts = jnp.stack([parts, exchange(parts, axis, masks[0])], axis=1)  3.06 us
  transfers between devices with their start and end apart: 11, of which 8 were waited for; matrix products, arithmetic and copies ran while one was open for 3% of the time, Pallas kernels for 0%

profile of v1, /device:TPU:0, one launch (start us, length us, event | category | flops | bytes accessed | tf_op | source)
XLA Modules:
  0.0 145.4 jit_solution(311508699011703508)
XLA Ops:
  7.2 1.5 %fusion.7 = (s32[1]{0:T(128)}, s32[1]{0:T(128)}, s32[1]{0:T(128)}, s32[1]{0:T(128)}) fusion(s32[32]{0:T(128)} %param.11), kind=kLoop, calls=%fused_computation.32 | loop fusion | bytes 32 | tf_op jit(solution)/shard_map/slice | solution.py:428
  16.4 0.7 fusion.4
  17.1 0.7 fusion.6
  17.8 3.5 %dynamic-slice_select_fusion.3 = (bf16[1,8,16,256]{3,2,1,0:T(8,128)(2,1)S(1)}, bf16[1,8,16,256]{3,2,1,0:T(8,128)(2,1)S(1)}, bf16[1,8,16,256]{3,2,1,0:T(8,128)(2,1)S(1)}, bf16[1,8,16,256]{3,2,1,0:T(8,128)(2,1)S(1)}) fusion(bf16[8,8,16,256]{3,2,1,0:T(8,128)(2,1)} %coher_ref.1, s32[]{:T(128)S(6)} %select_n.79, pred[]{:T(512)} %bitcast.5, s32[]{:T(128)S(6)} %select_n.87, ...), kind=kLoop, calls=%fused_computation.12 | loop fusion | flops 131072 | bytes 524308 | tf_op jit(solution)/shard_map/jit(_where)/select_n | solution.py:428
  21.3 3.1 %collective-permute-start.3 = (bf16[4,8,16,256]{3,2,1,0:T(8,128)(2,1)S(1)}, bf16[4,8,16,256]{3,2,1,0:T(8,128)(2,1)S(1)}, u32[]{:S(2)}, u32[]{:S(2)}) collective-permute-start(bf16[4,8,16,256]{3,2,1,0:T(8,128)(2,1)S(1)} %pad_maximum_fusion.3), channel_id=1, source_target_pairs={{0,1},{1,0},{2,3},{3,2},{4,5},{5,4},{6,7},{7,6},{8,9},{9,8},{10,11... | collective-permute-start | bytes 786440 | tf_op jit(solution)/shard_map/ppermute | solution.py:378
  24.4 0.7 compare_select_fusion.3
  25.2 0.9 copy-done.2
  26.1 0.6 pack_gains.1
  26.7 1.5 %collective-permute-start = (f32[1,48,128]{2,1,0:T(8,128)S(1)}, f32[1,48,128]{2,1,0:T(8,128)S(1)}, u32[]{:S(2)}, u32[]{:S(2)}) collective-permute-start(f32[1,48,128]{2,1,0:T(8,128)S(1)} %bitcast.22), channel_id=1, source_target_pairs={{0,8},{4,12},{8,0},{12,4},{16,24},{20,28},{24,16},{28,20},{1,9},{5... | collective-permute-start | bytes 73736 | tf_op jit(solution)/shard_map/ppermute | solution.py:378
  28.2 2.3 %collective-permute-done = f32[1,48,128]{2,1,0:T(8,128)S(1)} collective-permute-done((f32[1,48,128]{2,1,0:T(8,128)S(1)}, f32[1,48,128]{2,1,0:T(8,128)S(1)}, u32[]{:S(2)}, u32[]{:S(2)}) %collective-permute-start) | collective-permute-done | bytes 24608 | tf_op jit(solution)/shard_map/ppermute | solution.py:378
  30.5 1.5 %collective-permute-start.1 = (f32[2,48,128]{2,1,0:T(8,128)S(1)}, f32[2,48,128]{2,1,0:T(8,128)S(1)}, u32[]{:S(2)}, u32[]{:S(2)}) collective-permute-start(f32[2,48,128]{2,1,0:T(8,128)S(1)} %pad_maximum_fusion.6), channel_id=1, source_target_pairs={{0,16},{4,20},{8,24},{12,28},{16,0},{20,4},{24,8},{28,12},{1,17},{... | collective-permute-start | bytes 147464 | tf_op jit(solution)/shard_map/ppermute | solution.py:378
  32.1 2.7 %collective-permute-start.4 = (bf16[4,8,16,256]{3,2,1,0:T(8,128)(2,1)S(1)}, bf16[4,8,16,256]{3,2,1,0:T(8,128)(2,1)S(1)}, u32[]{:S(2)}, u32[]{:S(2)}) collective-permute-start(bf16[4,8,16,256]{3,2,1,0:T(8,128)(2,1)S(1)} %fusion.2), channel_id=1, source_target_pairs={{0,2},{1,3},{2,0},{3,1},{4,6},{5,7},{6,4},{7,5},{8,10},{9,11},{10,... | collective-permute-start | bytes 786440 | tf_op jit(solution)/shard_map/ppermute | solution.py:378
  34.9 1.2 collective-permute-done.2
  36.2 9.1 %collective-permute-done.4 = bf16[4,8,16,256]{3,2,1,0:T(8,128)(2,1)S(1)} collective-permute-done((bf16[4,8,16,256]{3,2,1,0:T(8,128)(2,1)S(1)}, bf16[4,8,16,256]{3,2,1,0:T(8,128)(2,1)S(1)}, u32[]{:S(2)}, u32[]{:S(2)}) %collective-permute-start.4) | collective-permute-done | bytes 262176 | tf_op jit(solution)/shard_map/ppermute | solution.py:378
  45.4 3.1 %first_model.1 = (f32[8,16,256]{2,1,0:T(8,128)S(1)}, f32[2,128,128]{2,1,0:T(8,128)S(1)}, f32[2,264,128]{2,1,0:T(8,128)S(1)}, f32[32,512]{1,0:T(8,128)S(1)}) custom-call(s32[1]{0:T(128)} %bitcast.base_ref, f32[4]{0:T(128)S(1)} %get-tuple-element.10.flag_ref, f32[8,48,128]{2,1,0:T(8,128)S(1)} %bitcast.21, s32[2,256]{1,0:T(2,128)S(1)} %copy-done.4, ...), custom_call_target="tpu_custom_call" | custom-call | tf_op jit(solution)/shard_map/first_model/pallas_call | solution.py:438
  48.6 0.2 collective-permute-start.5
  48.8 4.8 %collective-permute-done.5 = f32[2,128,128]{2,1,0:T(8,128)S(1)} collective-permute-done((f32[2,128,128]{2,1,0:T(8,128)S(1)}, f32[2,128,128]{2,1,0:T(8,128)S(1)}, u32[]{:S(2)}, u32[]{:S(2)}) %collective-permute-start.5) | collective-permute-done | bytes 131104 | tf_op jit(solution)/shard_map/ppermute | solution.py:378
  53.6 1.7 %collective-permute-start.6 = (f32[2,128,128]{2,1,0:T(8,128)S(1)}, f32[2,128,128]{2,1,0:T(8,128)S(1)}, u32[]{:S(2)}, u32[]{:S(2)}) collective-permute-start(f32[2,128,128]{2,1,0:T(8,128)S(1)} %add.69), channel_id=1, source_target_pairs={{0,2},{1,3},{2,0},{3,1},{4,6},{5,7},{6,4},{7,5},{8,10},{9,11},{10,... | collective-permute-start | bytes 393224 | tf_op jit(solution)/shard_map/ppermute | solution.py:378
  55.4 5.8 %collective-permute-done.6 = f32[2,128,128]{2,1,0:T(8,128)S(1)} collective-permute-done((f32[2,128,128]{2,1,0:T(8,128)S(1)}, f32[2,128,128]{2,1,0:T(8,128)S(1)}, u32[]{:S(2)}, u32[]{:S(2)}) %collective-permute-start.6) | collective-permute-done | bytes 131104 | tf_op jit(solution)/shard_map/ppermute | solution.py:378
  61.2 1.6 %collective-permute-start.7 = (f32[1,2,392,128]{3,2,1,0:T(8,128)S(1)}, f32[1,2,392,128]{3,2,1,0:T(8,128)S(1)}, u32[]{:S(2)}, u32[]{:S(2)}) collective-permute-start(f32[1,2,392,128]{3,2,1,0:T(8,128)S(1)} %maximum_bitcast_fusion), channel_id=1, source_target_pairs={{0,8},{4,12},{8,0},{12,4},{16,24},{20,28},{24,16},{28,20},{1,9},{5... | collective-permute-start | bytes 1204232 | tf_op jit(solution)/shard_map/ppermute | solution.py:378
  62.8 8.6 %collective-permute-done.7 = f32[1,2,392,128]{3,2,1,0:T(8,128)S(1)} collective-permute-done((f32[1,2,392,128]{3,2,1,0:T(8,128)S(1)}, f32[1,2,392,128]{3,2,1,0:T(8,128)S(1)}, u32[]{:S(2)}, u32[]{:S(2)}) %collective-permute-start.7) | collective-permute-done | bytes 401440 | tf_op jit(solution)/shard_map/ppermute | solution.py:378
  71.5 2.4 %collective-permute-start.8 = (f32[2,2,392,128]{3,2,1,0:T(8,128)S(1)}, f32[2,2,392,128]{3,2,1,0:T(8,128)S(1)}, u32[]{:S(2)}, u32[]{:S(2)}) collective-permute-start(f32[2,2,392,128]{3,2,1,0:T(8,128)S(1)} %pad_maximum_fusion.2), channel_id=1, source_target_pairs={{0,16},{4,20},{8,24},{12,28},{16,0},{20,4},{24,8},{28,12},{1,17},{... | collective-permute-start | bytes 2408456 | tf_op jit(solution)/shard_map/ppermute | solution.py:378
  73.9 16.2 %collective-permute-done.8 = f32[2,2,392,128]{3,2,1,0:T(8,128)S(1)} collective-permute-done((f32[2,2,392,128]{3,2,1,0:T(8,128)S(1)}, f32[2,2,392,128]{3,2,1,0:T(8,128)S(1)}, u32[]{:S(2)}, u32[]{:S(2)}) %collective-permute-start.8) | collective-permute-done | bytes 802848 | tf_op jit(solution)/shard_map/ppermute | solution.py:378
  90.1 1.4 fusion.3
  91.5 0.6 gather_fusion.1
  92.2 0.6 gather_fusion
  92.8 0.7 copy.15
  93.6 22.5 %reduce-scatter.2.cloned.1.call-done = f32[8,4,256]{2,0,1:T(8,128)} async-done(((f32[8,16,256]{2,0,1:T(8,128)}), f32[8,4,256]{2,0,1:T(8,128)}) %reduce-scatter.2.cloned.1.call-update) | async-done | bytes 32784 | tf_op jit(solution)/shard_map/reduce_scatter | solution.py:453
  116.1 0.8 copy.16.first_ref
  116.9 1.6 %pad_maximum_fusion = f32[4,2,2,392,128]{4,3,2,0,1:T(8,128)S(1)} fusion(f32[4,1,2,392,128]{4,3,2,0,1:T(8,128)} %bitcast.15, f32[4,1,2,392,128]{4,3,2,0,1:T(8,128)S(1)} %get-tuple-element.12), kind=kLoop, calls=%fused_computation.2 | loop fusion | flops 802816 | bytes 6422528 | tf_op jit(solution)/shard_map/stack | solution.py:395
  118.8 0.7 copy-done.3
  119.5 19.1 %sweep.1 = (f32[32,8,64]{2,1,0:T(8,128)}, f32[8,4,256]{2,1,0:T(4,128)}) custom-call(s32[1]{0:T(128)} %bitcast.base_ref, s32[4]{0:T(128)S(1)} %get-tuple-element.29.which_ref, s32[4]{0:T(128)S(1)} %broadcast_minimum_fusion.rounds_ref, f32[4]{0:T(128)S(1)} %convert_multiply_fusion.damp_ref, f32[6272,128]{1,0:T(8,128)S(1)} %bitcast.20, ...), custom_call_target="tpu_custom_call" | custom-call | tf_op jit(solution)/shard_map/sweep/pallas_call | solution.py:457
  (39 shorter events, 0.8 us)
Async XLA Ops:
  7.2 84.3 %copy-start = (s32[32]{0:T(128)S(1)}, s32[32]{0:T(128)}, u32[]{:S(2)}) copy-start(s32[32]{0:T(128)} %param.13) | copy-start | bytes 388
  7.2 27.7 %copy-start.6 = (f32[8,4,256]{2,1,0:T(4,128)S(1)}, f32[8,4,256]{2,1,0:T(4,128)}, u32[]{:S(2)}) copy-start(f32[8,4,256]{2,1,0:T(4,128)} %param.7) | copy-start | bytes 98308
  7.2 108.9 %reduce-scatter.2.cloned.1.call-start = ((), (), s32[]{:S(2)}) async-start(), calls=%async_computation.1 | async-start | bytes 163840 | tf_op jit(solution)/shard_map/reduce_scatter | solution.py:453
  21.3 10.7 %collective-permute-start.3 = (bf16[4,8,16,256]{3,2,1,0:T(8,128)(2,1)S(1)}, bf16[4,8,16,256]{3,2,1,0:T(8,128)(2,1)S(1)}, u32[]{:S(2)}, u32[]{:S(2)}) collective-permute-start(bf16[4,8,16,256]{3,2,1,0:T(8,128)(2,1)S(1)} %pad_maximum_fusion.3), channel_id=1, source_target_pairs={{0,1},{1,0},{2,3},{3,2},{4,5},{5,4},{6,7},{7,6},{8,9},{9,8},{10,11... | collective-permute-start | bytes 786440 | tf_op jit(solution)/shard_map/ppermute | solution.py:378
  25.2 0.9 copy-start.2
  26.7 3.8 %collective-permute-start = (f32[1,48,128]{2,1,0:T(8,128)S(1)}, f32[1,48,128]{2,1,0:T(8,128)S(1)}, u32[]{:S(2)}, u32[]{:S(2)}) collective-permute-start(f32[1,48,128]{2,1,0:T(8,128)S(1)} %bitcast.22), channel_id=1, source_target_pairs={{0,8},{4,12},{8,0},{12,4},{16,24},{20,28},{24,16},{28,20},{1,9},{5... | collective-permute-start | bytes 73736 | tf_op jit(solution)/shard_map/ppermute | solution.py:378
  28.2 17.2 %copy-start.1 = (bf16[8,8,16,256]{3,2,1,0:T(8,128)(2,1)S(1)}, bf16[8,8,16,256]{3,2,1,0:T(8,128)(2,1)}, u32[]{:S(2)}) copy-start(bf16[8,8,16,256]{3,2,1,0:T(8,128)(2,1)} %coher_ref.1) | copy-start | bytes 1572868
  28.2 17.2 %copy-start.4 = (s32[2,256]{1,0:T(2,128)S(1)}, s32[2,256]{1,0:T(2,128)}, u32[]{:S(2)}) copy-start(s32[2,256]{1,0:T(2,128)} %stations_ref.1) | copy-start | bytes 6148
  30.5 4.2 %collective-permute-start.1 = (f32[2,48,128]{2,1,0:T(8,128)S(1)}, f32[2,48,128]{2,1,0:T(8,128)S(1)}, u32[]{:S(2)}, u32[]{:S(2)}) collective-permute-start(f32[2,48,128]{2,1,0:T(8,128)S(1)} %pad_maximum_fusion.6), channel_id=1, source_target_pairs={{0,16},{4,20},{8,24},{12,28},{16,0},{20,4},{24,8},{28,12},{1,17},{... | collective-permute-start | bytes 147464 | tf_op jit(solution)/shard_map/ppermute | solution.py:378
  32.1 13.2 %collective-permute-start.4 = (bf16[4,8,16,256]{3,2,1,0:T(8,128)(2,1)S(1)}, bf16[4,8,16,256]{3,2,1,0:T(8,128)(2,1)S(1)}, u32[]{:S(2)}, u32[]{:S(2)}) collective-permute-start(bf16[4,8,16,256]{3,2,1,0:T(8,128)(2,1)S(1)} %fusion.2), channel_id=1, source_target_pairs={{0,2},{1,3},{2,0},{3,1},{4,6},{5,7},{6,4},{7,5},{8,10},{9,11},{10,... | collective-permute-start | bytes 786440 | tf_op jit(solution)/shard_map/ppermute | solution.py:378
  34.8 1.4 collective-permute-start.2
  48.6 5.0 %collective-permute-start.5 = (f32[2,128,128]{2,1,0:T(8,128)S(1)}, f32[2,128,128]{2,1,0:T(8,128)S(1)}, u32[]{:S(2)}, u32[]{:S(2)}) collective-permute-start(f32[2,128,128]{2,1,0:T(8,128)S(1)} %get-tuple-element.6), channel_id=1, source_target_pairs={{0,1},{1,0},{2,3},{3,2},{4,5},{5,4},{6,7},{7,6},{8,9},{9,8},{10,11... | collective-permute-start | bytes 393224 | tf_op jit(solution)/shard_map/ppermute | solution.py:378
  53.6 7.6 %collective-permute-start.6 = (f32[2,128,128]{2,1,0:T(8,128)S(1)}, f32[2,128,128]{2,1,0:T(8,128)S(1)}, u32[]{:S(2)}, u32[]{:S(2)}) collective-permute-start(f32[2,128,128]{2,1,0:T(8,128)S(1)} %add.69), channel_id=1, source_target_pairs={{0,2},{1,3},{2,0},{3,1},{4,6},{5,7},{6,4},{7,5},{8,10},{9,11},{10,... | collective-permute-start | bytes 393224 | tf_op jit(solution)/shard_map/ppermute | solution.py:378
  61.2 10.1 %collective-permute-start.7 = (f32[1,2,392,128]{3,2,1,0:T(8,128)S(1)}, f32[1,2,392,128]{3,2,1,0:T(8,128)S(1)}, u32[]{:S(2)}, u32[]{:S(2)}) collective-permute-start(f32[1,2,392,128]{3,2,1,0:T(8,128)S(1)} %maximum_bitcast_fusion), channel_id=1, source_target_pairs={{0,8},{4,12},{8,0},{12,4},{16,24},{20,28},{24,16},{28,20},{1,9},{5... | collective-permute-start | bytes 1204232 | tf_op jit(solution)/shard_map/ppermute | solution.py:378
  71.5 20.7 %copy-start.5 = (s32[32]{0:T(128)S(1)}, s32[32]{0:T(128)}, u32[]{:S(2)}) copy-start(s32[32]{0:T(128)} %param.12) | copy-start | bytes 388
  71.5 18.6 %collective-permute-start.8 = (f32[2,2,392,128]{3,2,1,0:T(8,128)S(1)}, f32[2,2,392,128]{3,2,1,0:T(8,128)S(1)}, u32[]{:S(2)}, u32[]{:S(2)}) collective-permute-start(f32[2,2,392,128]{3,2,1,0:T(8,128)S(1)} %pad_maximum_fusion.2), channel_id=1, source_target_pairs={{0,16},{4,20},{8,24},{12,28},{16,0},{20,4},{24,8},{28,12},{1,17},{... | collective-permute-start | bytes 2408456 | tf_op jit(solution)/shard_map/ppermute | solution.py:378
  91.5 25.4 %collective-permute-start.9 = (f32[4,2,392,128]{3,2,1,0:T(8,128)}, f32[4,2,392,128]{3,2,1,0:T(8,128)}, u32[]{:S(2)}, u32[]{:S(2)}) collective-permute-start(f32[4,2,392,128]{3,2,1,0:T(8,128)} %get-tuple-element.13), channel_id=1, source_target_pairs={{0,4},{4,0},{8,12},{12,8},{16,20},{20,16},{24,28},{28,24},{1,5},{5... | collective-permute-start | bytes 4816904 | tf_op jit(solution)/shard_map/ppermute | solution.py:378
  118.6 0.9 copy-start.3
Sparse Core Ops, SparseCore 0:
  93.7 22.3 reduce-scatter.1
